TPU v7x, 128 devices: a whole 4x4x4 slice. The times are simulated.
128 devices in a mesh: qr: 8 (over z_lo, x), kc: 16 (over y, z_hi, core).
Axes of the slice: x: 4, y: 4, z: 4 (z_hi: 2, z_lo: 2; z = z_hi * 2 + z_lo), core: 2. Of those that a mesh axis runs over, the one named last changes fastest.
Arguments:
- queries: bfloat16 [24576, 512], P(('qr', 'kc')), may hold values from -48 to 48, as said below
- keys: bfloat16 [24576, 512], P(('qr', 'kc')), may hold values from -16 to 16, as said below
- pair: int32 [24576], P(('qr', 'kc')), may hold values from 0 to 24575, each once
Outputs:
- loss: float32 [], replicated
- query_grad: float32 [24576, 512], P(('qr', 'kc'))
- key_grad: float32 [24576, 512], P(('qr', 'kc'))
Inputs may be any that keep to these rules, and one draw needn't show every extreme that they name: queries lie within this range; the shown draw within -6 to 6. keys lie within this range; the shown draw within -6 to 6. Every key is the pair of exactly one query.
All inputs are finite; a program needn't handle non-finite values.
Results may differ from a plain program's by a relative error of at most 0.0018.
Values may be sent and summed in bfloat16 or wider, within the bound.
A program may use at most 128 MiB of HBM per device.

v0:
```python
import math

import jax
import jax.numpy as jnp
from jax import lax
from jax.sharding import PartitionSpec as P


def shards(queries, keys, pair):
    qr_count = lax.axis_size("qr")
    kc_count = lax.axis_size("kc")
    rows_dev = queries.shape[0]
    width = queries.shape[1]
    pair_count = rows_dev * qr_count * kc_count
    factor = 2.0 / math.sqrt(width)
    query_rows, query_pair = (
        lax.all_gather(queries, "kc", axis=0, tiled=True),
        lax.all_gather(pair, "kc", axis=0, tiled=True),
    )
    key_rows = lax.all_gather(keys, "qr", axis=0, tiled=True)
    row_place = lax.axis_index("qr")
    col_place = lax.axis_index("kc")
    column = jnp.arange(key_rows.shape[0], dtype=jnp.int32)
    key_ids = (column // rows_dev * kc_count + col_place) * rows_dev + column % rows_dev
    height = math.gcd(query_rows.shape[0], 512)
    blocks = jnp.arange(query_rows.shape[0] // height, dtype=jnp.int32)

    def score_rows(first_row, row_count):
        query_block = lax.dynamic_slice_in_dim(query_rows, first_row, row_count, 0)
        pair_block = lax.dynamic_slice_in_dim(query_pair, first_row, row_count, 0)
        scores = (
            jnp.einsum("re,ce->rc", query_block, key_rows, preferred_element_type=jnp.float32)
            * factor
        )
        positive_mask = key_ids[None, :] == pair_block[:, None]
        return (query_block, scores, positive_mask)

    def forward(state_carry, number):
        col_peak, col_mass, positive = state_carry
        query_block, scores, positive_mask = score_rows(number * height, height)
        row_peak = jnp.max(scores, axis=1)
        row_mass = jnp.sum(jnp.exp(scores - row_peak[:, None]), axis=1)
        new_peak = jnp.maximum(col_peak, jnp.max(scores, axis=0))
        col_mass = col_mass * jnp.exp(col_peak - new_peak) + jnp.sum(
            jnp.exp(scores - new_peak[None, :]), axis=0
        )
        positive = positive + jnp.sum(jnp.where(positive_mask, scores, 0.0))
        return ((new_peak, col_mass, positive), (row_peak, row_mass))

    start_state = (
        jnp.full((key_rows.shape[0],), -jnp.inf, jnp.float32),
        jnp.zeros((key_rows.shape[0],), jnp.float32),
        jnp.zeros((), jnp.float32),
    )
    (col_peak, col_mass, positive), (row_peak, row_mass) = lax.scan(forward, start_state, blocks)
    row_peak = row_peak.reshape(-1)
    row_mass = row_mass.reshape(-1)
    row_top = lax.pmax(row_peak, "kc")
    row_sum = lax.psum(row_mass * jnp.exp(row_peak - row_top), "kc")
    col_top = lax.pmax(col_peak, "qr")
    col_sum = lax.psum(col_mass * jnp.exp(col_peak - col_top), "qr")
    lse_row = row_top + jnp.log(row_sum)
    lse_col = col_top + jnp.log(col_sum)
    own_rows = lax.dynamic_slice_in_dim(lse_row, col_place * rows_dev, rows_dev, 0)
    own_cols = lax.dynamic_slice_in_dim(lse_col, row_place * rows_dev, rows_dev, 0)
    partial_loss = jnp.sum(own_rows) + jnp.sum(own_cols) - 2.0 * positive
    grand_total = lax.psum(partial_loss, ("qr", "kc"))
    loss = grand_total / (2.0 * pair_count)

    def slope_rows(first_row, row_count):
        query_block, scores, positive_mask = score_rows(first_row, row_count)
        row_part = lax.dynamic_slice_in_dim(lse_row, first_row, row_count, 0)
        slopes = (
            (
                jnp.exp(scores - row_part[:, None])
                + jnp.exp(scores - lse_col[None, :])
                - jnp.where(positive_mask, 2.0, 0.0)
            )
            * 0.5
        ).astype(jnp.bfloat16)
        return (query_block, slopes)

    empty_keys = jnp.zeros((key_rows.shape[0], width), jnp.float32)

    def backward(key_grad, number):
        query_block, slopes = slope_rows(number * height, height)
        query_part = jnp.dot(slopes, key_rows, preferred_element_type=jnp.float32) * factor
        key_grad = (
            key_grad
            + jnp.einsum("rc,re->ce", slopes, query_block, preferred_element_type=jnp.float32)
            * factor
        )
        return (key_grad, query_part)

    key_terms, query_parts = lax.scan(backward, empty_keys, blocks)
    query_grad = lax.psum_scatter(
        query_parts.reshape(-1, width), "kc", scatter_dimension=0, tiled=True
    )
    key_grad = lax.psum_scatter(key_terms, "qr", scatter_dimension=0, tiled=True)
    return (loss, query_grad, key_grad)


def solution(mesh):
    placed = (P(("qr", "kc"), None), P(("qr", "kc"), None), P(("qr", "kc")))
    return jax.shard_map(
        shards,
        mesh=mesh,
        in_specs=placed,
        out_specs=(P(), P(("qr", "kc"), None), P(("qr", "kc"), None)),
        check_vma=False,
    )
```

profile of v0, /device:TPU:1, one launch (start us, length us, event | category | flops | bytes accessed | tf_op | source)
XLA Modules:
  0.0 518.4 jit_solution(3053186814378955946)
XLA Ops:
  7.2 0.7 all-gather.5.cloned.1.call-update
  7.9 0.7 all-gather.3.cloned.1.call-update
  8.8 1.2 dynamic-slice
  10.7 0.9 dynamic-update-slice
  11.6 66.4 %all-reduce = s32[3072]{0:T(1024)S(1)} all-reduce(s32[3072]{0:T(1024)S(1)} %dynamic-update-slice), channel_id=1, replica_groups=mesh['qr'=8,'kc'=16] {'kc'}, use_global_device_ids=true, to_apply=%add | all-reduce | flops 3072 | bytes 24576
  77.9 30.1 %all-gather.3.cloned.1.call-done = bf16[3072,512]{1,0:T(8,128)(2,1)} async-done(((bf16[192,512]{1,0:T(8,128)(2,1)}), bf16[3072,512]{1,0:T(8,128)(2,1)}) %all-gather.3.cloned.1.call-update) | async-done | bytes 3145744 | tf_op jit(solution)/shard_map/all_gather | solution.py:17
  108.0 44.6 %while.32 = (s32[]{:T(128)}, f32[1536]{0:T(1024)S(1)}, f32[1536]{0:T(1024)S(1)}, f32[]{:T(128)}, f32[6,512]{1,0:T(8,128)S(1)}, /*index=5*/f32[6,512]{1,0:T(8,128...) while((s32[]{:T(128)}, f32[1536]{0:T(1024)S(1)}, ...), condition=%wide.region_6.7_spmd.clone, body=%wide.region_0.6_spmd.clone.sunk | while | flops 813201920 | bytes 8501502 | solution.py:55
  108.0 0.6 dynamic_slice.56
  109.4 2.7 fusion.56
  112.1 2.6 exponential_reduce_fusion.3
  115.5 0.6 dynamic_slice.56
  116.7 0.1 dynamic_slice.57
  116.8 2.7 fusion.56
  119.5 2.6 exponential_reduce_fusion.3
  122.9 0.6 dynamic_slice.56
  124.1 0.1 dynamic_slice.57
  124.2 2.7 fusion.56
  126.9 2.6 exponential_reduce_fusion.3
  130.3 0.6 dynamic_slice.56
  131.6 0.1 dynamic_slice.57
  131.7 2.7 fusion.56
  134.4 2.6 exponential_reduce_fusion.3
  137.8 0.6 dynamic_slice.56
  139.0 0.1 dynamic_slice.57
  139.1 2.7 fusion.56
  141.8 2.6 exponential_reduce_fusion.3
  145.2 0.6 dynamic_slice.56
  146.5 2.7 fusion.56
  149.2 2.6 exponential_reduce_fusion.3
  152.6 15.2 %pmax.15 = f32[1536]{0:T(1024)S(1)} all-reduce(f32[1536]{0:T(1024)S(1)} %get-tuple-element.119), channel_id=1, replica_groups=mesh['qr'=8,'kc'=16] {'qr'}, use_global_device_ids=true, to_apply=%region_10.11 | all-reduce | flops 1536 | bytes 12288 | tf_op jit(solution)/shard_map/pmax | solution.py:60
  167.9 12.7 %psum.22 = f32[1536]{0:T(1024)S(1)} all-reduce(f32[1536]{0:T(1024)S(1)} %exponential_multiply_fusion.1), channel_id=1, replica_groups=mesh['qr'=8,'kc'=16] {'qr'}, use_global_device_ids=true, to_apply=%region_11.12 | all-reduce | flops 1536 | bytes 12288 | tf_op jit(solution)/shard_map/psum | solution.py:61
  180.6 66.5 %pmax.14 = f32[3072]{0:T(1024)S(1)} all-reduce(f32[3072]{0:T(1024)S(1)} %reshape.27), channel_id=1, replica_groups=mesh['qr'=8,'kc'=16] {'kc'}, use_global_device_ids=true, to_apply=%region_7.8 | all-reduce | flops 3072 | bytes 24576 | tf_op jit(solution)/shard_map/pmax | solution.py:58
  247.1 64.9 %psum.21 = f32[3072]{0:T(1024)S(1)} all-reduce(f32[3072]{0:T(1024)S(1)} %exponential_multiply_fusion), channel_id=1, replica_groups=mesh['qr'=8,'kc'=16] {'kc'}, use_global_device_ids=true, to_apply=%region_8.9 | all-reduce | flops 3072 | bytes 24576 | tf_op jit(solution)/shard_map/psum | solution.py:59
  312.1 56.1 %while.33 = (s32[]{:T(128)}, f32[1536,512]{1,0:T(8,128)S(1)}, f32[6,512,512]{2,1,0:T(8,128)}, s32[6]{0:T(128)S(1)}, bf16[3072,512]{1,0:T(8,128)(2,1)}, /*index=5...) while((s32[]{:T(128)}, f32[1536,512]{1,0:T(8,128)S(1)}, ...), condition=%wide.region_15.16_spmd.clone, body=%wide.region_14.15_spmd.clone.sunk | while | flops 2425643008 | bytes 22575364 | solution.py:95
  312.1 0.6 dynamic_slice.60
  313.5 3.4 multiply_convert_fusion.2
  316.9 2.6 fusion.66
  319.5 2.0 fusion.67
  321.4 0.6 dynamic_slice.60
  322.9 3.3 multiply_convert_fusion.2
  326.2 2.6 fusion.66
  328.8 2.0 fusion.67
  330.8 0.6 dynamic_slice.60
  332.2 3.3 multiply_convert_fusion.2
  335.6 2.6 fusion.66
  338.2 2.0 fusion.67
  340.2 0.6 dynamic_slice.60
  341.6 3.3 multiply_convert_fusion.2
  344.9 2.6 fusion.66
  347.5 2.0 fusion.67
  349.5 0.6 dynamic_slice.60
  350.9 3.4 multiply_convert_fusion.2
  354.3 2.6 fusion.66
  356.8 2.0 fusion.67
  358.8 0.6 dynamic_slice.60
  360.2 3.4 multiply_convert_fusion.2
  363.6 2.6 fusion.66
  366.2 2.0 fusion.67
  368.2 1.7 copy-done
  369.9 0.5 reduce-scatter.3.cloned.1.call-update
  370.5 0.7 dynamic-slice_reduce_fusion
  371.2 0.7 dynamic-slice_reduce_fusion.1
  373.2 78.1 %psum.23 = f32[]{:T(128)} all-reduce(f32[]{:T(128)S(6)} %sub.56), channel_id=1, replica_groups=mesh['qr'=8,'kc'=16] {'qr','kc'}, use_global_device_ids=true, to_apply=%region_13.14 | all-reduce | flops 1 | bytes 8 | tf_op jit(solution)/shard_map/psum | solution.py:67
  451.9 58.8 %reduce-scatter.3.cloned.1.call-done = f32[192,512]{1,0:T(8,128)} async-done(((f32[3072,512]{1,0:T(8,128)}), f32[192,512]{1,0:T(8,128)}) %reduce-scatter.3.cloned.1.call-update) | async-done | bytes 393232 | tf_op jit(solution)/shard_map/reduce_scatter | solution.py:96
  (91 shorter events, 2.4 us)
Async XLA Ops:
  7.2 70.8 %all-gather.5.cloned.1.call-start = ((), (), s32[]{:S(2)}) async-start(), calls=%async_computation.3 | async-start | bytes 1769472 | tf_op jit(solution)/shard_map/all_gather | solution.py:20
  7.9 100.1 %all-gather.3.cloned.1.call-start = ((), (), s32[]{:S(2)}) async-start(), calls=%async_computation.2 | async-start | bytes 3342336 | tf_op jit(solution)/shard_map/all_gather | solution.py:17
  8.6 443.3 %reduce-scatter.5.cloned.1.call-start = ((), (), s32[]{:S(2)}) async-start(), calls=%async_computation.5 | async-start | bytes 3538944 | tf_op jit(solution)/shard_map/reduce_scatter | solution.py:99
  316.9 2.6 copy-start.1
  326.2 2.6 copy-start.1
  335.6 2.6 copy-start.1
  344.9 2.6 copy-start.1
  354.2 2.6 copy-start.1
  363.6 2.6 copy-start.1
  368.2 1.7 copy-start
  369.9 140.8 %reduce-scatter.3.cloned.1.call-start = ((), (), s32[]{:S(2)}) async-start(), calls=%async_computation.4 | async-start | bytes 6684672 | tf_op jit(solution)/shard_map/reduce_scatter | solution.py:96
Sparse Core Ops, SparseCore 0:
  9.6 38.7 all-gather.4
  50.9 57.1 all-gather.2
  370.0 44.4 reduce-scatter.4
  419.0 91.6 reduce-scatter.2
where the time goes:
time: 520 us; the launch traced here: 518 us
  blocking collectives  304 us (58%)
  waiting for transfers between devices  90.8 us (17%)
  matrix products  63.5 us (12%)
  between operations  17.6 us (3%)
  other arithmetic  17.1 us (3%)
  local copies, waits for them, and re-layouts  13 us (2%)
  loops' own time  12.3 us (2%)
    psum x1, blocking collectives, shards(): grand_total = lax.psum(partial_loss, ('qr', 'kc'))  78.1 us
    pmax x1, blocking collectives, shards(): row_top = lax.pmax(row_peak, 'kc')  66.5 us
    unnamed x1, blocking collectives  66.4 us
    psum x1, blocking collectives, shards(): row_sum = lax.psum(row_mass * jnp.exp(row_peak - row_top), 'kc')  64.9 us
    reduce_scatter x1, waiting for transfers between devices, shards(): lax.psum_scatter(query_parts.reshape(-1, width), 'kc', scatter_dimension=...  58.8 us
    dot_general x12, matrix products, score_rows(): jnp.einsum('re,ce->rc', query_block, key_rows, preferred_element_type=jnp...  36.2 us
    all_gather x1, waiting for transfers between devices, shards(): lax.all_gather(queries, 'kc', axis=0, tiled=True)  30.1 us
    dot_general x6, matrix products, backward(): jnp.einsum('rc,re->ce', slopes, query_block, preferred_element_type=jnp.f...  15.4 us
  transfers between devices with their start and end apart: 4, of which 2 were waited for; matrix products, arithmetic and copies ran while one was open for 1% of the time, Pallas kernels for 0%

commit v1 on v0

v1 whole, which is shorter than its diff:
```python
import functools
import math

import jax
import jax.numpy as jnp
from jax import lax
from jax.experimental import pallas as pl
from jax.experimental.pallas import tpu as pltpu
from jax.sharding import PartitionSpec as P

MESH = pl.DeviceIdType.MESH
LOG2E = math.log2(math.e)
LN2 = math.log(2.0)
QR = 8
KC = 16
B = 192
PB = 2 * B
WIDTH = 512
ROWS = KC * B
COLS = QR * B
CHUNK = 768
LANES = 128


def rows(start, size, step=16):
    return pl.ds(pl.multiple_of(start, step), size)


def nt_dot(a, b):
    return lax.dot_general(a, b, (((1,), (1,)), ((), ())), preferred_element_type=jnp.float32)


def tn_dot(a, b):
    return lax.dot_general(a, b, (((0,), (0,)), ((), ())), preferred_element_type=jnp.float32)


def kernel(
    q_ref, k_ref, pair_ref, loss_ref, qg_ref, kg_ref,
    q_all, k_all, scores, slopes, q_sum, k_sum,
    pair_own, pair_all, pair_col,
    row_send, row_recv, row_lse, col_max, col_mass, col_send, col_recv, col_lse,
    loss_a, loss_b, positive, core_recv,
    q_code, q_step, q_code_in, q_step_in, k_code, k_step, k_code_in, k_step_in,
    gather_send, gather_recv, core_send_sem, core_recv_sem,
    q_code_send, q_code_recv, q_step_send, q_step_recv, k_code_send, k_code_recv, k_step_send, k_step_recv,
    small_send, small_recv,
):
    r = lax.axis_index("qr")
    c = lax.axis_index("kc")
    zl, x = r // 4, r % 4
    y, zh, core = c // 4, (c // 2) % 2, c % 2
    factor2 = 2.0 / math.sqrt(WIDTH) * LOG2E
    factor = 2.0 / math.sqrt(WIDTH)

    def kc_dev(yy, zz, cc):
        return (r, yy * 4 + zz * 2 + cc)

    def qr_dev(zz, xx):
        return (zz * 4 + xx, c)

    def copy(src, dst, send, recv, device):
        return pltpu.make_async_remote_copy(
            src_ref=src, dst_ref=dst, send_sem=send, recv_sem=recv,
            device_id=device, device_id_type=MESH,
        )

    barrier = pltpu.get_barrier_semaphore()

    @pl.loop(1, KC)
    def _(o):
        pl.semaphore_signal(barrier, inc=1, device_id=(r, (c + o) % KC), device_id_type=MESH)

    @pl.loop(1, QR)
    def _(o):
        pl.semaphore_signal(barrier, inc=1, device_id=((r + o) % QR, c), device_id_type=MESH)

    pl.semaphore_wait(barrier, KC + QR - 2)

    yu, yd, yo = (y + 1) % 4, (y + 3) % 4, (y + 2) % 4
    xu, xd, xo = (x + 1) % 4, (x + 3) % 4, (x + 2) % 4
    zhp, zlp, corep = 1 - zh, 1 - zl, 1 - core
    H = B // 2

    def q_rows(yy, zz, cc):
        return (zz * 8 + yy * 2 + cc) * B

    def k_rows(xx, zz):
        return (zz * 4 + xx) * B

    def q_lane(yy, zz):
        return q_rows(yy, zz, core)

    q_ring = (kc_dev(yu, zh, core), kc_dev(yd, zh, core), kc_dev(y, zhp, core))
    k_ring = (qr_dev(zl, xu), qr_dev(zl, xd), qr_dev(zlp, x))

    def gather_copy(buf, base, n, start, size, device, src=None):
        view = buf.at[rows(start, size)]
        return copy(view if src is None else src, view, gather_send.at[base + n], gather_recv.at[base + n], device)

    def make_gather(buf, own, base, slot, ring, here, up, down, far, z, zp):
        to_up, to_down, to_pair = ring
        send = {
            0: gather_copy(buf, base, 0, slot(here, z), B, to_up, own),
            1: gather_copy(buf, base, 1, slot(here, z), B, to_down, own),
            2: gather_copy(buf, base, 2, slot(here, z), B, to_pair, own),
            3: gather_copy(buf, base, 3, slot(down, z), H, to_up),
            4: gather_copy(buf, base, 4, slot(up, z) + H, H, to_down),
            5: gather_copy(buf, base, 5, slot(here, zp), B, to_up),
            6: gather_copy(buf, base, 6, slot(here, zp), B, to_down),
            7: gather_copy(buf, base, 7, slot(down, zp), H, to_up),
            8: gather_copy(buf, base, 8, slot(up, zp) + H, H, to_down),
        }
        recv = {
            0: gather_copy(buf, base, 0, slot(down, z), B, to_up),
            1: gather_copy(buf, base, 1, slot(up, z), B, to_up),
            2: gather_copy(buf, base, 2, slot(here, zp), B, to_up),
            3: gather_copy(buf, base, 3, slot(far, z), H, to_up),
            4: gather_copy(buf, base, 4, slot(far, z) + H, H, to_up),
            5: gather_copy(buf, base, 5, slot(down, zp), B, to_up),
            6: gather_copy(buf, base, 6, slot(up, zp), B, to_up),
            7: gather_copy(buf, base, 7, slot(far, zp), H, to_up),
            8: gather_copy(buf, base, 8, slot(far, zp) + H, H, to_up),
        }
        return send, recv

    k_out, k_in = make_gather(k_all, k_ref, 0, k_rows, k_ring, x, xu, xd, xo, zl, zlp)
    q_out, q_in = make_gather(q_all, q_ref, 9, q_lane, q_ring, y, yu, yd, yo, zh, zhp)
    sibling = kc_dev(y, zh, corep)
    lane_slots = ((y, zh), (yd, zh), (yu, zh), (y, zhp), (yo, zh), (yd, zhp), (yu, zhp), (yo, zhp))
    swap_out = [
        gather_copy(q_all, 18, n, q_rows(yy, zz, core), B, sibling, q_ref if n == 0 else None)
        for n, (yy, zz) in enumerate(lane_slots)
    ]
    swap_in = [
        gather_copy(q_all, 18, n, q_rows(yy, zz, corep), B, sibling) for n, (yy, zz) in enumerate(lane_slots)
    ]

    for n in (0, 1, 2):
        k_out[n].start()
        q_out[n].start()
    swap_out[0].start()

    def pair_copy(o):
        return copy(pair_own, pair_all.at[c], small_send.at[o], small_recv.at[o], (r, (c + o) % KC))

    pair_own[...] = jnp.zeros((1, 2 * LANES), jnp.int32)
    pair_own[:, 0:B] = pair_ref[...]

    @pl.loop(1, KC)
    def _(o):
        pair_copy(o).start()

    q_all[rows(q_rows(y, zh, core), B), :] = q_ref[...]
    k_all[rows(k_rows(x, zl), B), :] = k_ref[...]
    pair_all[c] = pair_own[...]

    for arrived, started in ((0, (3,)), (1, (4,)), (2, (5, 6))):
        k_in[arrived].wait_recv()
        for n in started:
            k_out[n].start()
        q_in[arrived].wait_recv()
        for n in started:
            q_out[n].start()
        swap_out[arrived + 1].start()
    for n in (3, 4):
        k_in[n].wait_recv()
        q_in[n].wait_recv()
    swap_out[4].start()
    for arrived, started in ((5, 7), (6, 8)):
        k_in[arrived].wait_recv()
        k_out[started].start()
        q_in[arrived].wait_recv()
        q_out[started].start()
        swap_out[arrived].start()

    @pl.loop(1, KC)
    def _(o):
        pair_copy(o).wait_recv()

    @pl.loop(0, KC)
    def _(k):
        wide = jnp.broadcast_to(pair_all[k].astype(jnp.float32), (LANES, 2 * LANES)).T
        pair_col[rows(q_rows(k // 4, (k // 2) % 2, k % 2), B), :] = wide[:B].astype(jnp.int32)

    for n in (7, 8):
        k_in[n].wait_recv()
        q_in[n].wait_recv()
    swap_out[7].start()
    for n in range(8):
        swap_in[n].wait_recv()

    col_max[...] = jnp.full((1, COLS), -1e30, jnp.float32)
    col_mass[...] = jnp.zeros((1, COLS), jnp.float32)

    @pl.loop(0, ROWS // PB)
    def _(p):
        here = rows(p * PB, PB)
        block = q_all[here, :]
        peak = None
        for n in range(COLS // CHUNK):
            cols = pl.ds(n * CHUNK, CHUNK)
            s = nt_dot(block, k_all[cols, :]) * factor2
            scores[here, cols] = s
            top = jnp.max(s, axis=0, keepdims=True)
            mass = jnp.sum(jnp.exp2(s - top), axis=0, keepdims=True)
            old = col_max[:, cols]
            new = jnp.maximum(old, top)
            col_max[:, cols] = new
            col_mass[:, cols] = col_mass[:, cols] * jnp.exp2(old - new) + mass * jnp.exp2(top - new)
            for g in range(CHUNK // LANES):
                part = s[:, g * LANES:(g + 1) * LANES]
                peak = part if peak is None else jnp.maximum(peak, part)
        peak = jnp.broadcast_to(jnp.max(peak, axis=1, keepdims=True), (PB, LANES))
        mass = None
        for g in range(COLS // LANES):
            e = jnp.exp2(scores[here, pl.ds(g * LANES, LANES)] - peak)
            mass = e if mass is None else mass + e
        row_send[pl.ds(p, 1), :] = peak.T[0:1, :] + jnp.log(jnp.sum(mass.T, axis=0, keepdims=True)) * LOG2E

    col_send[...] = col_max[...] + jnp.log(col_mass[...]) * LOG2E

    def row_copy(o):
        return copy(row_send, row_recv.at[c], small_send.at[KC + o], small_recv.at[KC + o], (r, (c + o) % KC))

    def col_copy(o):
        return copy(col_send, col_recv.at[r], small_send.at[2 * KC + o], small_recv.at[2 * KC + o], ((r + o) % QR, c))

    @pl.loop(1, KC)
    def _(o):
        row_copy(o).start()

    @pl.loop(1, QR)
    def _(o):
        col_copy(o).start()

    row_recv[c] = row_send[...]
    col_recv[r] = col_send[...]

    def combine(recv, count):
        top = recv[0]
        for n in range(1, count):
            top = jnp.maximum(top, recv[n])
        mass = jnp.zeros_like(top)
        for n in range(count):
            mass = mass + jnp.exp2(recv[n] - top)
        return top + jnp.log(mass) * LOG2E

    @pl.loop(1, KC)
    def _(o):
        row_copy(o).wait_recv()

    row_lse[...] = combine(row_recv, KC)

    @pl.loop(1, QR)
    def _(o):
        col_copy(o).wait_recv()

    col_lse[...] = combine(col_recv, QR)

    def encode(code, step, n, value):
        unit = jnp.maximum(jnp.max(jnp.abs(value), axis=0, keepdims=True), 1e-33) * (1.0 / 32766.0)
        code[n] = jnp.round(value * (1.0 / unit)).astype(jnp.int32).astype(jnp.int16)
        step[n] = unit

    def make_reduce(buf, slot, ring, own_z, other_z, code, step, code_in, step_in, sems, here, up, down, far):
        to_up, to_down, to_pair = ring
        code_send, code_recv, step_send, step_recv = sems

        def copies(n, device):
            return (
                copy(code.at[n], code_in.at[n], code_send.at[n], code_recv.at[n], device),
                copy(step.at[n], step_in.at[n], step_send.at[n], step_recv.at[n], device),
            )

        def send(n, value, device):
            encode(code, step, n, value)
            for one in copies(n, device):
                one.start()

        def take(n):
            for one in copies(n, to_up):
                one.wait_recv()
            return code_in[n].astype(jnp.int32).astype(jnp.float32) * step_in[n]

        def half(s, place, bottom):
            return rows(slot(place, other_z if s == 0 else own_z) + (H if bottom else 0), H)

        def first(s):
            send(6 * s, buf[half(s, far, False), :], to_up)
            send(6 * s + 1, buf[half(s, far, True), :], to_down)

        def raw_up(s):
            send(6 * s + 2, buf[half(s, up, True), :], to_up)

        def raw_down(s):
            send(6 * s + 3, buf[half(s, down, False), :], to_down)

        def pass_up(s):
            send(6 * s + 4, buf[half(s, up, False), :] + take(6 * s), to_up)

        def pass_down(s):
            send(6 * s + 5, buf[half(s, down, True), :] + take(6 * s + 1), to_down)

        def final(s, bottom):
            mine = buf[half(s, here, bottom), :]
            if bottom:
                return mine + take(6 * s + 2) + take(6 * s + 5)
            return mine + take(6 * s + 3) + take(6 * s + 4)

        def pair_send():
            for n, bottom in ((12, False), (13, True)):
                send(n, final(0, bottom), to_pair)

        def result(out):
            for n, bottom in ((12, False), (13, True)):
                out[pl.ds(H if bottom else 0, H), :] = (final(1, bottom) + take(n)) * factor

        def drain():
            @pl.loop(0, 14)
            def _(n):
                for one in copies(n, to_up):
                    one.wait_send()

        return first, raw_up, raw_down, pass_up, pass_down, pair_send, result, drain

    q_first, q_raw_up, q_raw_down, q_pass_up, q_pass_down, q_pair, q_result, q_drain = make_reduce(
        q_sum, q_lane, q_ring, zh, zhp, q_code, q_step, q_code_in, q_step_in,
        (q_code_send, q_code_recv, q_step_send, q_step_recv), y, yu, yd, yo)
    k_first, k_raw_up, k_raw_down, k_pass_up, k_pass_down, k_pair, k_result, k_drain = make_reduce(
        k_sum, k_rows, k_ring, zl, zlp, k_code, k_step, k_code_in, k_step_in,
        (k_code_send, k_code_recv, k_step_send, k_step_recv), x, xu, xd, xo)

    positive[...] = jnp.zeros((8, LANES), jnp.float32)
    lane = lax.broadcasted_iota(jnp.int32, (1, LANES), 1)

    def key_ids(zz, g):
        low = (g * LANES) // B
        high = (g * LANES + LANES - 1) // B
        column = lane + (g * LANES + zz * 4 * B * KC + c * B)
        ids = column + low * (KC - 1) * B
        if low == high:
            return ids
        return jnp.where(lane + g * LANES >= high * B, column + high * (KC - 1) * B, ids)

    def step_place(t):
        return (y + jnp.where(t == 0, 2, jnp.where(t == 1, 1, jnp.where(t == 2, 3, 0)))) % 4

    def make_slopes(p, groups):
        here = rows(p * PB, PB)
        row_part = jnp.broadcast_to(row_lse[pl.ds(p, 1), :] + 1.0, (LANES, PB)).T
        pairs = pair_col[here, :]
        found = None
        for zz in groups:
            for g in range(CHUNK // LANES):
                cols = pl.ds(pl.multiple_of(zz * CHUNK + g * LANES, LANES), LANES)
                s = scores[here, cols]
                mask = key_ids(zz, g) == pairs
                z = jnp.exp2(s - row_part) + jnp.exp2(s - (col_lse[:, cols] + 1.0)) - jnp.where(mask, 1.0, 0.0)
                slopes[here, cols] = z.astype(jnp.bfloat16)
                hit = jnp.where(mask, s, 0.0)
                found = hit if found is None else found + hit
        positive[...] = positive[...] + jnp.sum(found.reshape(PB // 8, 8, LANES), axis=0)

    def core_out(zz, yy):
        n = zz * 4 + yy
        return copy(q_sum.at[rows(q_rows(yy, zz, corep), B)], core_recv.at[n], core_send_sem.at[n], core_recv_sem.at[n], sibling)

    def core_add(zz, yy):
        core_out(zz, yy).wait_recv()
        here = rows(q_lane(yy, zz), B)
        q_sum[here, :] = q_sum[here, :] + core_recv[zz * 4 + yy]

    def query_product(s, with_slopes):
        zz = zhp if s == 0 else zh

        @pl.loop(0, 4)
        def _(t):
            yy = step_place(t)
            p = zz * 4 + yy
            here = rows(p * PB, PB)
            if with_slopes:
                make_slopes(p, (0, 1))
            q_sum[here, :] = jnp.dot(slopes[here, :], k_all[...], preferred_element_type=jnp.float32)
            core_out(zz, yy).start()

            @pl.when(t > 0)
            def _():
                core_add(zz, step_place(t - 1))

            @pl.when(t == 1)
            def _():
                q_first(s)

            @pl.when(t == 2)
            def _():
                q_raw_up(s)

            @pl.when(t == 3)
            def _():
                q_raw_down(s)
                q_pass_up(s)

        core_add(zz, y)
        q_pass_down(s)

    def key_product(s):
        zz = zlp if s == 0 else zl
        cols = pl.ds(pl.multiple_of(zz * CHUNK, LANES), CHUNK)
        k_sum[rows(zz * CHUNK, CHUNK), :] = tn_dot(slopes[:, cols], q_all[...])

    def own_slopes(zz):
        @pl.loop(0, 4)
        def _(t):
            make_slopes(zh * 4 + t, (zz,))

    query_product(0, True)
    own_slopes(zlp)
    key_product(0)
    k_first(0)
    k_raw_up(0)
    k_raw_down(0)
    own_slopes(zl)

    share = jnp.sum(positive[...], axis=0, keepdims=True) * (-2.0)
    rows_lse = row_lse[pl.ds(zh * 4 + y, 1), :]
    for g in range(PB // LANES):
        share = share + jnp.where(core == 0, rows_lse[:, g * LANES:(g + 1) * LANES], 0.0)
    for g in range(CHUNK // LANES):
        cols = pl.ds(pl.multiple_of(zl * CHUNK + g * LANES, LANES), LANES)
        share = share + jnp.where(x == 0, col_lse[:, cols], 0.0)
    loss_a[c] = share

    def loss_copy_a(o):
        return copy(loss_a.at[c], loss_a.at[c], small_send.at[40 + o], small_recv.at[40 + o], (r, (c + o) % KC))

    def loss_copy_b(o):
        return copy(loss_b.at[r], loss_b.at[r], small_send.at[56 + o], small_recv.at[56 + o], ((r + o) % QR, c))

    @pl.loop(1, KC)
    def _(o):
        loss_copy_a(o).start()

    k_pass_up(0)
    k_pass_down(0)
    key_product(1)
    k_first(1)
    k_raw_up(1)
    k_raw_down(1)
    q_pair()
    query_product(1, False)
    k_pass_up(1)
    k_pass_down(1)

    @pl.loop(1, KC)
    def _(o):
        loss_copy_a(o).wait_recv()

    total = loss_a[0]
    for n in range(1, KC):
        total = total + loss_a[n]
    loss_b[r] = total

    @pl.loop(1, QR)
    def _(o):
        loss_copy_b(o).start()

    k_pair()
    q_result(qg_ref)
    k_result(kg_ref)

    @pl.loop(1, QR)
    def _(o):
        loss_copy_b(o).wait_recv()

    total = loss_b[0]
    for n in range(1, QR):
        total = total + loss_b[n]
    loss_ref[...] = jnp.sum(total, axis=1, keepdims=True) * (LN2 / (2.0 * QR * KC * B))

    for n in range(9):
        k_out[n].wait_send()
        q_out[n].wait_send()
    for n in range(8):
        swap_out[n].wait_send()

    @pl.loop(1, KC)
    def _(o):
        pair_copy(o).wait_send()
        row_copy(o).wait_send()
        loss_copy_a(o).wait_send()

    @pl.loop(1, QR)
    def _(o):
        col_copy(o).wait_send()
        loss_copy_b(o).wait_send()

    @pl.loop(0, 8)
    def _(n):
        core_out(n // 4, n % 4).wait_send()

    q_drain()
    k_drain()


def finish(loss_in, query_in, key_in, loss_ref, query_ref, key_ref):
    loss_ref[...] = loss_in[...]
    query_ref[...] = query_in[...]
    key_ref[...] = key_in[...]


def shards(queries, keys, pair):
    pair = pair.reshape(1, B)
    f32, bf16 = jnp.float32, jnp.bfloat16
    vmem = pl.BlockSpec(memory_space=pltpu.VMEM)
    dma = pltpu.SemaphoreType.DMA
    loss, query_grad, key_grad = pl.pallas_call(
        kernel,
        out_shape=(
            jax.ShapeDtypeStruct((1, 1), f32),
            jax.ShapeDtypeStruct((B, WIDTH), f32),
            jax.ShapeDtypeStruct((B, WIDTH), f32),
        ),
        in_specs=[vmem] * 3,
        out_specs=(vmem,) * 3,
        scratch_shapes=[
            pltpu.VMEM((ROWS, WIDTH), bf16),
            pltpu.VMEM((COLS, WIDTH), bf16),
            pltpu.VMEM((ROWS, COLS), f32),
            pltpu.VMEM((ROWS, COLS), bf16),
            pltpu.VMEM((ROWS, WIDTH), f32),
            pltpu.VMEM((COLS, WIDTH), f32),
            pltpu.VMEM((1, 2 * LANES), jnp.int32),
            pltpu.VMEM((KC, 1, 2 * LANES), jnp.int32),
            pltpu.VMEM((ROWS, LANES), jnp.int32),
            pltpu.VMEM((8, PB), f32),
            pltpu.VMEM((KC, 8, PB), f32),
            pltpu.VMEM((8, PB), f32),
            pltpu.VMEM((1, COLS), f32),
            pltpu.VMEM((1, COLS), f32),
            pltpu.VMEM((1, COLS), f32),
            pltpu.VMEM((QR, 1, COLS), f32),
            pltpu.VMEM((1, COLS), f32),
            pltpu.VMEM((KC, 1, LANES), f32),
            pltpu.VMEM((QR, 1, LANES), f32),
            pltpu.VMEM((8, LANES), f32),
            pltpu.VMEM((8, B, WIDTH), f32),
        ]
        + [pltpu.VMEM((14, B // 2, WIDTH), jnp.int16), pltpu.VMEM((14, 1, WIDTH), f32)] * 4
        + [dma((26,)), dma((26,)), dma((8,)), dma((8,))]
        + [dma((14,))] * 8
        + [dma((64,)), dma((64,))],
        compiler_params=pltpu.CompilerParams(
            collective_id=0, has_side_effects=True, vmem_limit_bytes=60 * 1024 * 1024
        ),
    )(queries, keys, pair)
    loss, query_grad, key_grad = pl.pallas_call(
        finish,
        out_shape=(
            jax.ShapeDtypeStruct((1, 1), f32),
            jax.ShapeDtypeStruct((B, WIDTH), f32),
            jax.ShapeDtypeStruct((B, WIDTH), f32),
        ),
        in_specs=[vmem] * 3,
        out_specs=(vmem,) * 3,
    )(loss, query_grad, key_grad)
    return loss.reshape(()), query_grad, key_grad


def solution(mesh):
    placed = (P(("qr", "kc"), None), P(("qr", "kc"), None), P(("qr", "kc")))
    return jax.shard_map(
        shards,
        mesh=mesh,
        in_specs=placed,
        out_specs=(P(), P(("qr", "kc"), None), P(("qr", "kc"), None)),
        check_vma=False,
    )
```

time: 520 us -> 92.7 us (0.18)
  blocking collectives: 304 us -> 0 us
  Pallas kernels: 0 us -> 91.9 us
  waiting for transfers between devices: 90.8 us -> 0 us
  matrix products: 63.5 us -> 0 us
  other arithmetic: 17.1 us -> 0 us
  between operations: 17.6 us -> 0.64 us
  local copies, waits for them, and re-layouts: 13 us -> 0 us
  loops' own time: 12.3 us -> 0 us
    psum x3 -> x0, blocking collectives: 156 us -> none  [the longest x1 78.1 us: shards(): grand_total = lax.psum(partial_loss, ('qr', 'kc'))]
    pallas_call x0 -> x2, Pallas kernels: none -> 91.9 us  [the longest x1 89.3 us: shards(): pl.pallas_call(kernel, out_shape=(jax.ShapeDtypeStruct((1, 1), f32), jax....]
    pmax x2 -> x0, blocking collectives: 81.7 us -> none  [the longest x1 66.5 us: shards(): row_top = lax.pmax(row_peak, 'kc')]
    unnamed x1 -> x0, blocking collectives: 66.4 us -> none
    dot_general x24 -> x0, matrix products: 63.5 us -> none  [the longest x12 36.2 us: score_rows(): jnp.einsum('re,ce->rc', query_block, key_rows, preferred_element_type=jnp...]
    reduce_scatter x2 -> x0, waiting for transfers between devices: 58.8 us -> none  [the longest x1 58.8 us: shards(): lax.psum_scatter(query_parts.reshape(-1, width), 'kc', scatter_dimension=...]
    all_gather x2 -> x0, waiting for transfers between devices: 30.1 us -> none  [the longest x1 30.1 us: shards(): lax.all_gather(queries, 'kc', axis=0, tiled=True)]
    reduce_sum x8 -> x0, other arithmetic: 16.8 us -> none  [the longest x6 15.4 us: forward(): row_mass = jnp.sum(jnp.exp(scores - row_peak[:, None]), axis=1)]
  transfers between devices with their start and end apart: 4 -> 0, of which waited for: 2 -> 0; matrix products, arithmetic and copies ran while one was open for 1% -> 0% of each run, Pallas kernels for 0% -> 0%
where the time goes in v1:
time: 92.7 us; the launch traced here: 92.5 us
  Pallas kernels  91.9 us (99%)
    pallas_call x1, Pallas kernels, shards(): pl.pallas_call(kernel, out_shape=(jax.ShapeDtypeStruct((1, 1), f32), jax....  89.3 us
    pallas_call x1, Pallas kernels, shards(): pl.pallas_call(finish, out_shape=(jax.ShapeDtypeStruct((1, 1), f32), jax....  2.66 us

profile of v1, /device:TPU:1, one launch (start us, length us, event | category | flops | bytes accessed | tf_op | source)
XLA Modules:
  0.0 92.5 jit_solution(2897306779800820987)
XLA Ops:
  0.6 89.3 %shard_map.58 = (f32[1,1]{1,0:T(1,128)}, f32[192,512]{1,0:T(8,128)}, f32[192,512]{1,0:T(8,128)}) custom-call(bf16[192,512]{1,0:T(8,128)(2,1)} %q_ref.1, bf16[192,512]{1,0:T(8,128)(2,1)} %k_ref.1, s32[1,192]{1,0:T(1,128)} %bitcast.2), custom_call_target="tpu_custom_call" | custom-call | tf_op jit(solution)/shard_map/pallas_call | solution.py:516
  89.9 2.7 %shard_map.59 = (f32[1,1]{1,0:T(1,128)}, f32[192,512]{1,0:T(8,128)}, f32[192,512]{1,0:T(8,128)}) custom-call(f32[1,1]{1,0:T(1,128)} %get-tuple-element.9.loss_in, f32[192,512]{1,0:T(8,128)} %get-tuple-element.10.query_in, f32[192,512]{1,0:T(8,128)} %get-tuple-element.11.key_in), custom_call_target="tpu_custom_call" | custom-call | tf_op jit(solution)/shard_map/pallas_call | solution.py:556

commit v2 on v1

v2 whole, which is shorter than its diff:
```python
import functools
import math

import jax
import jax.numpy as jnp
from jax import lax
from jax.experimental import pallas as pl
from jax.experimental.pallas import tpu as pltpu
from jax.sharding import PartitionSpec as P

MESH = pl.DeviceIdType.MESH
LOG2E = math.log2(math.e)
LN2 = math.log(2.0)
QR = 8
KC = 16
B = 192
PB = 2 * B
WIDTH = 512
ROWS = KC * B
COLS = QR * B
CHUNK = 768
LANES = 128
FACTOR = 2.0 / math.sqrt(WIDTH)


def rows(start, size, step=16):
    return pl.ds(pl.multiple_of(start, step), size)


def nt_dot(a, b):
    return lax.dot_general(a, b, (((1,), (1,)), ((), ())), preferred_element_type=jnp.float32)


def tn_dot(a, b):
    return lax.dot_general(a, b, (((0,), (0,)), ((), ())), preferred_element_type=jnp.float32)


def kernel(
    q_ref, k_ref, pair_ref, loss_ref, qg_ref, kg_ref,
    q_all, k_all, scores, slopes, q_sum, k_sum,
    pair_own, pair_all, pair_col,
    row_part, row_send, row_recv, row_lse, row_col, col_max, col_mass, col_send, col_recv, col_lse,
    loss_a, loss_b, positive, core_recv,
    q_code, q_step, q_code_in, q_step_in, k_code, k_step, k_code_in, k_step_in,
    own_sem, gather_send, gather_recv, core_send_sem, core_recv_sem,
    q_code_send, q_code_recv, q_step_send, q_step_recv, k_code_send, k_code_recv, k_step_send, k_step_recv,
    small_send, small_recv,
):
    r = lax.axis_index("qr")
    c = lax.axis_index("kc")
    zl, x = r // 4, r % 4
    y, zh, core = c // 4, (c // 2) % 2, c % 2
    factor2 = FACTOR * LOG2E

    def kc_dev(yy, zz, cc):
        return (r, yy * 4 + zz * 2 + cc)

    def qr_dev(zz, xx):
        return (zz * 4 + xx, c)

    def copy(src, dst, send, recv, device):
        return pltpu.make_async_remote_copy(
            src_ref=src, dst_ref=dst, send_sem=send, recv_sem=recv,
            device_id=device, device_id_type=MESH,
        )

    y, zh, core = c // 4, (c // 2) % 2, c % 2
    yu, yd, yo = (y + 1) % 4, (y + 3) % 4, (y + 2) % 4
    xu, xd, xo = (x + 1) % 4, (x + 3) % 4, (x + 2) % 4
    zhp, zlp, corep = 1 - zh, 1 - zl, 1 - core
    q_ring = (kc_dev(yu, zh, core), kc_dev(yd, zh, core), kc_dev(y, zhp, core))
    k_ring = (qr_dev(zl, xu), qr_dev(zl, xd), qr_dev(zlp, x))
    sibling = kc_dev(y, zh, corep)
    barrier = pltpu.get_barrier_semaphore()
    for near in q_ring + k_ring + (sibling,):
        pl.semaphore_signal(barrier, inc=1, device_id=near, device_id_type=MESH)
    pl.semaphore_wait(barrier, 7)

    H = B // 2

    def q_rows(yy, zz, cc):
        return (zz * 8 + yy * 2 + cc) * B

    def k_rows(xx, zz):
        return (zz * 4 + xx) * B

    def q_lane(yy, zz):
        return q_rows(yy, zz, core)

    def gather_copy(buf, n, start, size, device, src=None):
        view = buf.at[rows(start, size)]
        return copy(view if src is None else src, view, gather_send.at[n], gather_recv.at[n], device)

    def make_gather(buf, own, base, slot, ring, here, up, down, far, z, zp):
        to_up, to_down, to_pair = ring
        send, recv = {}, {}
        for h in range(2):
            half = own.at[pl.ds(h * H, H)]
            mine = slot(here, z) + h * H
            pairs = slot(here, zp) + h * H
            send[h] = gather_copy(buf, base + h, mine, H, to_up, half)
            send[2 + h] = gather_copy(buf, base + 2 + h, mine, H, to_down, half)
            send[4 + h] = gather_copy(buf, base + 4 + h, mine, H, to_pair, half)
            send[8 + h] = gather_copy(buf, base + 8 + h, pairs, H, to_up)
            send[10 + h] = gather_copy(buf, base + 10 + h, pairs, H, to_down)
            recv[h] = gather_copy(buf, base + h, slot(down, z) + h * H, H, to_up)
            recv[2 + h] = gather_copy(buf, base + 2 + h, slot(up, z) + h * H, H, to_up)
            recv[4 + h] = gather_copy(buf, base + 4 + h, pairs, H, to_up)
            recv[8 + h] = gather_copy(buf, base + 8 + h, slot(down, zp) + h * H, H, to_up)
            recv[10 + h] = gather_copy(buf, base + 10 + h, slot(up, zp) + h * H, H, to_up)
        for n, zz in ((6, z), (12, zp)):
            send[n] = gather_copy(buf, base + n, slot(down, zz), H, to_up)
            send[n + 1] = gather_copy(buf, base + n + 1, slot(up, zz) + H, H, to_down)
            recv[n] = gather_copy(buf, base + n, slot(far, zz), H, to_up)
            recv[n + 1] = gather_copy(buf, base + n + 1, slot(far, zz) + H, H, to_up)

        def start(*numbers):
            for n in numbers:
                send[n].start()

        def arrived(*numbers):
            for n in numbers:
                recv[n].wait_recv()

        def drain():
            for n in range(14):
                send[n].wait_send()

        return start, arrived, drain

    k_start, k_arrived, k_gather_drain = make_gather(k_all, k_ref, 0, k_rows, k_ring, x, xu, xd, xo, zl, zlp)
    q_start, q_arrived, q_gather_drain = make_gather(q_all, q_ref, 14, q_lane, q_ring, y, yu, yd, yo, zh, zhp)

    def ring_place(t):
        return (y + jnp.where(t == 0, 0, jnp.where(t == 1, 1, jnp.where(t == 2, 3, 2)))) % 4

    def swap_copy(s, t, cc):
        start = q_rows(ring_place(t), jnp.where(s == 0, zh, zhp), cc)
        src = q_ref if isinstance(s, int) and (s, t) == (0, 0) else None
        return gather_copy(q_all, 28 + s * 4 + t, start, B, sibling, src)

    def swap_start(s, t):
        swap_copy(s, t, core).start()

    def swap_arrived(s, t):
        swap_copy(s, t, corep).wait_recv()

    own_copies = (
        pltpu.make_async_copy(q_ref, q_all.at[rows(q_rows(y, zh, core), B)], own_sem.at[0]),
        pltpu.make_async_copy(k_ref, k_all.at[rows(k_rows(x, zl), B)], own_sem.at[1]),
    )
    k_start(4, 5)
    k_start(0, 3, 1, 2)
    q_start(0, 3, 1, 2)
    q_start(4, 5)
    swap_start(0, 0)
    for one in own_copies:
        one.start()
    pair_own[...] = jnp.zeros((1, 2 * LANES), jnp.int32)
    pair_own[:, 0:B] = pair_ref[...]
    col_max[...] = jnp.full((2, 1, CHUNK), -1e30, jnp.float32)
    col_mass[...] = jnp.zeros((2, 1, CHUNK), jnp.float32)
    for one in own_copies:
        one.wait()

    def lanes(g):
        return pl.ds(g * LANES, LANES)

    def score_unit(p, zz):
        here = rows(p * PB, PB)
        scores[zz, here, :] = nt_dot(q_all[here, :], k_all[rows(zz * CHUNK, CHUNK), :]) * factor2
        peak, tops = None, []
        for g in range(CHUNK // LANES):
            s = scores[zz, here, lanes(g)]
            peak = s if peak is None else jnp.maximum(peak, s)
            tops.append(jnp.max(s, axis=0, keepdims=True))
        peak = jnp.broadcast_to(jnp.max(peak, axis=1, keepdims=True), (PB, LANES))
        mass = None
        for g in range(CHUNK // LANES):
            s = scores[zz, here, lanes(g)]
            e = jnp.exp2(s - peak)
            mass = e if mass is None else mass + e
            new_mass = jnp.sum(jnp.exp2(s - tops[g]), axis=0, keepdims=True)
            old = col_max[zz, :, lanes(g)]
            new = jnp.maximum(old, tops[g])
            col_max[zz, :, lanes(g)] = new
            col_mass[zz, :, lanes(g)] = col_mass[zz, :, lanes(g)] * jnp.exp2(old - new) + new_mass * jnp.exp2(tops[g] - new)
        row_part[zz, pl.ds(p, 1), :] = peak.T[0:1, :] + jnp.log(jnp.sum(mass.T, axis=0, keepdims=True)) * LOG2E

    k_arrived(0)
    k_start(6)
    k_arrived(3)
    k_start(7)
    q_arrived(0)
    q_start(6)
    q_arrived(3)
    q_start(7)
    k_arrived(4)
    k_start(8, 10)
    k_arrived(1, 2)
    q_arrived(1, 2)
    swap_start(0, 1)
    swap_start(0, 2)
    k_arrived(5)
    k_start(9, 11)
    q_arrived(4)
    q_start(8, 10)
    k_arrived(6, 7)
    q_arrived(6, 7)
    swap_start(0, 3)
    swap_arrived(0, 0)

    def pair_copy(o):
        return copy(pair_own, pair_all.at[c], small_send.at[o], small_recv.at[o], (r, (c + o) % KC))

    def before_unit_1():
        k_arrived(8)
        k_start(12)
        q_arrived(5)
        q_start(9, 11)
        swap_start(1, 0)
        swap_arrived(0, 1)

    def before_unit_2():
        k_arrived(11)
        k_start(13)
        swap_arrived(0, 2)

    def before_unit_3():
        q_arrived(8)
        q_start(12)
        swap_arrived(0, 3)

    def before_unit_5():
        q_arrived(11)
        q_start(13)
        q_arrived(9, 10)
        swap_start(1, 1)
        swap_start(1, 2)
        k_arrived(9, 10, 12, 13)

    def before_unit_7():
        q_arrived(12, 13)
        swap_start(1, 3)

    def before_unit_14():
        swap_arrived(1, 3)

        @pl.loop(1, KC)
        def _(o):
            pair_copy(o).start()

    score_events = {
        1: before_unit_1, 2: before_unit_2, 3: before_unit_3, 4: lambda: swap_arrived(1, 0), 5: before_unit_5,
        7: before_unit_7, 10: lambda: swap_arrived(1, 1), 12: lambda: swap_arrived(1, 2), 14: before_unit_14,
    }

    for u in range(16):
        if u in score_events:
            score_events[u]()
        s, t, partner = (
            (0, 0, 0), (0, 1, 0), (0, 2, 0), (0, 3, 0), (1, 0, 0), (0, 0, 1), (0, 1, 1), (0, 2, 1), (0, 3, 1), (1, 0, 1),
            (1, 1, 0), (1, 1, 1), (1, 2, 0), (1, 2, 1), (1, 3, 0), (1, 3, 1),
        )[u]
        score_unit((zhp if s else zh) * 4 + ring_place(t), zlp if partner else zl)

    parts_top = jnp.maximum(row_part[0], row_part[1])
    parts_mass = jnp.exp2(row_part[0] - parts_top) + jnp.exp2(row_part[1] - parts_top)
    row_send[...] = parts_top + jnp.log(parts_mass) * LOG2E
    col_send[...] = col_max[...] + jnp.log(col_mass[...]) * LOG2E

    def row_copy(o):
        return copy(row_send, row_recv.at[c], small_send.at[KC + o], small_recv.at[KC + o], (r, (c + o) % KC))

    def col_copy(o):
        return copy(col_send, col_recv.at[r], small_send.at[2 * KC + o], small_recv.at[2 * KC + o], ((r + o) % QR, c))

    @pl.loop(1, KC)
    def _(o):
        row_copy(o).start()

    @pl.loop(1, QR)
    def _(o):
        col_copy(o).start()

    row_recv[c] = row_send[...]
    col_recv[r] = col_send[...]
    pair_all[c] = pair_own[...]

    @pl.loop(1, KC)
    def _(o):
        pair_copy(o).wait_recv()

    @pl.loop(0, KC)
    def _(k):
        wide = jnp.broadcast_to(pair_all[k].astype(jnp.float32), (LANES, 2 * LANES)).T
        pair_col[rows(q_rows(k // 4, (k // 2) % 2, k % 2), B), :] = wide[:B].astype(jnp.int32)

    def combine(recv, count):
        top = recv[0]
        for n in range(1, count):
            top = jnp.maximum(top, recv[n])
        mass = jnp.zeros_like(top)
        for n in range(count):
            mass = mass + jnp.exp2(recv[n] - top)
        return top + jnp.log(mass) * LOG2E

    @pl.loop(1, KC)
    def _(o):
        row_copy(o).wait_recv()

    row_lse[...] = combine(row_recv, KC)

    @pl.loop(0, 8)
    def _(p):
        row_col[rows(p * PB, PB), :] = jnp.broadcast_to(row_lse[pl.ds(p, 1), :] + 1.0, (LANES, PB)).T

    @pl.loop(1, QR)
    def _(o):
        col_copy(o).wait_recv()

    col_lse[...] = combine(col_recv, QR)

    def encode(code, step, n, value):
        unit = jnp.maximum(jnp.max(jnp.abs(value), axis=0, keepdims=True), 1e-33) * (1.0 / 32766.0)
        code[n] = jnp.round(value * (1.0 / unit)).astype(jnp.int32).astype(jnp.int16)
        step[n] = unit

    def make_reduce(buf, slot, ring, own_z, other_z, code, step, code_in, step_in, sems, here, up, down, far):
        to_up, to_down, to_pair = ring
        code_send, code_recv, step_send, step_recv = sems

        def copies(n, device):
            return (
                copy(code.at[n], code_in.at[n], code_send.at[n], code_recv.at[n], device),
                copy(step.at[n], step_in.at[n], step_send.at[n], step_recv.at[n], device),
            )

        def send(n, value, device):
            encode(code, step, n, value)
            for one in copies(n, device):
                one.start()

        def take(n):
            for one in copies(n, to_up):
                one.wait_recv()
            return code_in[n].astype(jnp.int32).astype(jnp.float32) * step_in[n]

        def half(s, place, bottom):
            return rows(slot(place, other_z if s == 0 else own_z) + (H if bottom else 0), H)

        def first(s):
            send(6 * s, buf[half(s, far, False), :], to_up)
            send(6 * s + 1, buf[half(s, far, True), :], to_down)

        def raw_up(s):
            send(6 * s + 2, buf[half(s, up, True), :], to_up)

        def raw_down(s):
            send(6 * s + 3, buf[half(s, down, False), :], to_down)

        def pass_up(s):
            send(6 * s + 4, buf[half(s, up, False), :] + take(6 * s), to_up)

        def pass_down(s):
            send(6 * s + 5, buf[half(s, down, True), :] + take(6 * s + 1), to_down)

        def final(s, bottom):
            mine = buf[half(s, here, bottom), :]
            if bottom:
                return mine + take(6 * s + 2) + take(6 * s + 5)
            return mine + take(6 * s + 3) + take(6 * s + 4)

        def pair_send():
            for n, bottom in ((12, False), (13, True)):
                send(n, final(0, bottom), to_pair)

        def result(out):
            for n, bottom in ((12, False), (13, True)):
                out[pl.ds(H if bottom else 0, H), :] = final(1, bottom) + take(n)

        def drain():
            @pl.loop(0, 14)
            def _(n):
                for one in copies(n, to_up):
                    one.wait_send()

        return first, raw_up, raw_down, pass_up, pass_down, pair_send, result, drain

    q_first, q_raw_up, q_raw_down, q_pass_up, q_pass_down, q_pair, q_result, q_drain = make_reduce(
        q_sum, q_lane, q_ring, zh, zhp, q_code, q_step, q_code_in, q_step_in,
        (q_code_send, q_code_recv, q_step_send, q_step_recv), y, yu, yd, yo)
    k_first, k_raw_up, k_raw_down, k_pass_up, k_pass_down, k_pair, k_result, k_drain = make_reduce(
        k_sum, k_rows, k_ring, zl, zlp, k_code, k_step, k_code_in, k_step_in,
        (k_code_send, k_code_recv, k_step_send, k_step_recv), x, xu, xd, xo)

    positive[...] = jnp.zeros((8, LANES), jnp.float32)
    lane = lax.broadcasted_iota(jnp.int32, (1, LANES), 1)

    def key_ids(zz, g):
        low = (g * LANES) // B
        high = (g * LANES + LANES - 1) // B
        column = lane + (g * LANES + zz * 4 * B * KC + c * B)
        ids = column + low * (KC - 1) * B
        if low == high:
            return ids
        return jnp.where(lane + g * LANES >= high * B, column + high * (KC - 1) * B, ids)

    def step_place(t):
        return (y + jnp.where(t == 0, 2, jnp.where(t == 1, 1, jnp.where(t == 2, 3, 0)))) % 4

    strip = LANES

    def make_slopes(p, zz):
        @pl.loop(0, PB // strip)
        def _(i):
            here = rows(p * PB + i * strip, strip)
            peak = row_col[here, :]
            pairs = pair_col[here, :]
            found = jnp.zeros((8, LANES), jnp.float32)
            for g in range(CHUNK // LANES):
                s = scores[zz, here, lanes(g)]
                mask = key_ids(zz, g) == pairs
                z = jnp.exp2(s - peak) + jnp.exp2(s - (col_lse[zz, :, lanes(g)] + 1.0)) - jnp.where(mask, 1.0, 0.0)
                slopes[zz, here, lanes(g)] = z.astype(jnp.bfloat16)
                found = found + jnp.sum(jnp.where(mask, s, 0.0).reshape(strip // 8, 8, LANES), axis=0)
            positive[...] = positive[...] + found

    def core_out(zz, yy):
        n = zz * 4 + yy
        return copy(q_sum.at[rows(q_rows(yy, zz, corep), B)], core_recv.at[n], core_send_sem.at[n], core_recv_sem.at[n], sibling)

    def core_add(zz, yy):
        core_out(zz, yy).wait_recv()
        here = rows(q_lane(yy, zz), B)
        q_sum[here, :] = q_sum[here, :] + core_recv[zz * 4 + yy]

    def tile_place(k):
        return (zhp + k // 4) % 2, step_place(k % 4)

    def slope_unit(u):
        k = jnp.where(u == 0, 0, jnp.where(u < 9, u - 1, u - 8))
        zz, yy = tile_place(k)
        make_slopes(zz * 4 + yy, (zl + jnp.where((u >= 1) & (u < 9), 1, 0)) % 2)

    def add_tile(k):
        core_add(*tile_place(k))

    def slope_units(low, high):
        @pl.loop(low, high)
        def _(u):
            slope_unit(u)

    def query_tile(k):
        zz, yy = tile_place(k)
        here = rows((zz * 4 + yy) * PB, PB)
        q_sum[here, :] = (
            jnp.dot(slopes[0, here, :], k_all[pl.ds(0, CHUNK), :], preferred_element_type=jnp.float32)
            + jnp.dot(slopes[1, here, :], k_all[pl.ds(CHUNK, CHUNK), :], preferred_element_type=jnp.float32)
        )
        core_out(zz, yy).start()

    def key_tile(zz, half):
        cols = pl.ds(pl.multiple_of(half * PB, LANES), PB)
        k_sum[rows(zz * CHUNK + half * PB, PB), :] = tn_dot(slopes[zz, :, cols], q_all[...])

    far_half, near_half = 1 - x // 2, x // 2
    slope_units(0, 2)
    query_tile(0)
    slope_units(2, 9)
    add_tile(0)
    q_first(0)
    key_tile(zlp, far_half)
    k_first(0)
    slope_units(9, 10)
    query_tile(1)
    slope_units(10, 11)
    query_tile(2)
    add_tile(1)
    q_raw_up(0)
    key_tile(zlp, near_half)
    k_raw_up(0)
    k_raw_down(0)
    add_tile(2)
    q_raw_down(0)
    slope_units(11, 16)
    share = jnp.sum(positive[...], axis=0, keepdims=True) * (-2.0)
    rows_lse = row_lse[pl.ds(zh * 4 + y, 1), :]
    for g in range(PB // LANES):
        share = share + jnp.where(core == 0, rows_lse[:, g * LANES:(g + 1) * LANES], 0.0)
    for g in range(CHUNK // LANES):
        share = share + jnp.where(x == 0, col_lse[zl, :, lanes(g)], 0.0)
    loss_a[c] = share

    def loss_copy_a(o):
        return copy(loss_a.at[c], loss_a.at[c], small_send.at[40 + o], small_recv.at[40 + o], (r, (c + o) % KC))

    def loss_copy_b(o):
        return copy(loss_b.at[r], loss_b.at[r], small_send.at[56 + o], small_recv.at[56 + o], ((r + o) % QR, c))

    @pl.loop(1, KC)
    def _(o):
        loss_copy_a(o).start()

    q_pass_up(0)
    q_pass_down(0)
    query_tile(4)
    k_pass_up(0)
    k_pass_down(0)
    key_tile(zl, far_half)
    add_tile(4)
    q_first(1)
    k_first(1)
    query_tile(3)
    query_tile(5)
    add_tile(3)
    query_tile(6)
    add_tile(5)
    q_raw_up(1)
    key_tile(zl, near_half)
    k_raw_up(1)
    k_raw_down(1)
    @pl.loop(1, KC)
    def _(o):
        loss_copy_a(o).wait_recv()

    total = loss_a[0]
    for n in range(1, KC):
        total = total + loss_a[n]
    loss_b[r] = total

    @pl.loop(1, QR)
    def _(o):
        loss_copy_b(o).start()

    add_tile(6)
    q_raw_down(1)
    q_pair()
    query_tile(7)
    k_pair()

    q_pass_up(1)
    q_pass_down(1)
    k_pass_up(1)
    k_pass_down(1)
    add_tile(7)

    k_result(kg_ref)
    q_result(qg_ref)

    @pl.loop(1, QR)
    def _(o):
        loss_copy_b(o).wait_recv()

    total = loss_b[0]
    for n in range(1, QR):
        total = total + loss_b[n]
    loss_ref[...] = jnp.sum(total, axis=1, keepdims=True) * (LN2 / (2.0 * QR * KC * B))

    k_gather_drain()
    q_gather_drain()
    for s in range(2):
        for t in range(4):
            swap_copy(s, t, core).wait_send()

    @pl.loop(1, KC)
    def _(o):
        pair_copy(o).wait_send()
        row_copy(o).wait_send()
        loss_copy_a(o).wait_send()

    @pl.loop(1, QR)
    def _(o):
        col_copy(o).wait_send()
        loss_copy_b(o).wait_send()

    @pl.loop(0, 8)
    def _(n):
        core_out(n // 4, n % 4).wait_send()

    q_drain()
    k_drain()


def finish(loss_in, query_in, key_in, loss_ref, query_ref, key_ref):
    loss_ref[...] = loss_in[...]
    query_ref[...] = query_in[...] * FACTOR
    key_ref[...] = key_in[...] * FACTOR


def shards(queries, keys, pair):
    pair = pair.reshape(1, B)
    f32, bf16 = jnp.float32, jnp.bfloat16
    vmem = pl.BlockSpec(memory_space=pltpu.VMEM)
    dma = pltpu.SemaphoreType.DMA
    loss, query_grad, key_grad = pl.pallas_call(
        kernel,
        out_shape=(
            jax.ShapeDtypeStruct((1, 1), f32),
            jax.ShapeDtypeStruct((B, WIDTH), f32),
            jax.ShapeDtypeStruct((B, WIDTH), f32),
        ),
        in_specs=[pl.BlockSpec(memory_space=pl.ANY)] * 2 + [vmem],
        out_specs=(vmem,) * 3,
        scratch_shapes=[
            pltpu.VMEM((ROWS, WIDTH), bf16),
            pltpu.VMEM((COLS, WIDTH), bf16),
            pltpu.VMEM((2, ROWS, CHUNK), f32),
            pltpu.VMEM((2, ROWS, CHUNK), bf16),
            pltpu.VMEM((ROWS, WIDTH), f32),
            pltpu.VMEM((COLS, WIDTH), f32),
            pltpu.VMEM((1, 2 * LANES), jnp.int32),
            pltpu.VMEM((KC, 1, 2 * LANES), jnp.int32),
            pltpu.VMEM((ROWS, LANES), jnp.int32),
            pltpu.VMEM((2, 8, PB), f32),
            pltpu.VMEM((8, PB), f32),
            pltpu.VMEM((KC, 8, PB), f32),
            pltpu.VMEM((8, PB), f32),
            pltpu.VMEM((ROWS, LANES), f32),
            pltpu.VMEM((2, 1, CHUNK), f32),
            pltpu.VMEM((2, 1, CHUNK), f32),
            pltpu.VMEM((2, 1, CHUNK), f32),
            pltpu.VMEM((QR, 2, 1, CHUNK), f32),
            pltpu.VMEM((2, 1, CHUNK), f32),
            pltpu.VMEM((KC, 1, LANES), f32),
            pltpu.VMEM((QR, 1, LANES), f32),
            pltpu.VMEM((8, LANES), f32),
            pltpu.VMEM((8, B, WIDTH), f32),
        ]
        + [pltpu.VMEM((14, B // 2, WIDTH), jnp.int16), pltpu.VMEM((14, 1, WIDTH), f32)] * 4
        + [dma((2,)), dma((36,)), dma((36,)), dma((8,)), dma((8,))]
        + [dma((14,))] * 8
        + [dma((64,)), dma((64,))],
        compiler_params=pltpu.CompilerParams(
            collective_id=0, has_side_effects=True, vmem_limit_bytes=60 * 1024 * 1024
        ),
    )(queries, keys, pair)
    loss, query_grad, key_grad = pl.pallas_call(
        finish,
        out_shape=(
            jax.ShapeDtypeStruct((1, 1), f32),
            jax.ShapeDtypeStruct((B, WIDTH), f32),
            jax.ShapeDtypeStruct((B, WIDTH), f32),
        ),
        in_specs=[vmem] * 3,
        out_specs=(vmem,) * 3,
    )(loss, query_grad, key_grad)
    return loss.reshape(()), query_grad, key_grad


def solution(mesh):
    placed = (P(("qr", "kc"), None), P(("qr", "kc"), None), P(("qr", "kc")))
    return jax.shard_map(
        shards,
        mesh=mesh,
        in_specs=placed,
        out_specs=(P(), P(("qr", "kc"), None), P(("qr", "kc"), None)),
        check_vma=False,
    )
```

time: 92.7 us -> 81.9 us (0.88)
  Pallas kernels: 91.9 us -> 81.1 us
    pallas_call x1, Pallas kernels: 89.3 us -> 78.4 us  [shards(): pl.pallas_call(kernel, out_shape=(jax.ShapeDtypeStruct((1, 1), f32), jax....]
where the time goes in v2:
time: 81.9 us; the launch traced here: 81.7 us
  Pallas kernels  81.1 us (99%)
    pallas_call x1, Pallas kernels, shards(): pl.pallas_call(kernel, out_shape=(jax.ShapeDtypeStruct((1, 1), f32), jax....  78.4 us
    pallas_call x1, Pallas kernels, shards(): pl.pallas_call(finish, out_shape=(jax.ShapeDtypeStruct((1, 1), f32), jax....  2.7 us

profile of v2, /device:TPU:1, one launch (start us, length us, event | category | flops | bytes accessed | tf_op | source)
XLA Modules:
  0.0 81.7 jit_solution(9230061597408210719)
XLA Ops:
  0.6 78.4 %shard_map.58 = (f32[1,1]{1,0:T(1,128)}, f32[192,512]{1,0:T(8,128)}, f32[192,512]{1,0:T(8,128)}) custom-call(bf16[192,512]{1,0:T(8,128)(2,1)} %q_ref.1, bf16[192,512]{1,0:T(8,128)(2,1)} %k_ref.1, s32[1,192]{1,0:T(1,128)} %bitcast.2), custom_call_target="tpu_custom_call" | custom-call | tf_op jit(solution)/shard_map/pallas_call | solution.py:596
  79.0 2.7 %shard_map.59 = (f32[1,1]{1,0:T(1,128)}, f32[192,512]{1,0:T(8,128)}, f32[192,512]{1,0:T(8,128)}) custom-call(f32[1,1]{1,0:T(1,128)} %get-tuple-element.9.loss_in, f32[192,512]{1,0:T(8,128)} %get-tuple-element.10.query_in, f32[192,512]{1,0:T(8,128)} %get-tuple-element.11.key_in), custom_call_target="tpu_custom_call" | custom-call | tf_op jit(solution)/shard_map/pallas_call | solution.py:638

commit v3 on v2

--- a/solution.py
+++ b/solution.py
@@ -409,7 +409,7 @@
     def step_place(t):
         return (y + jnp.where(t == 0, 2, jnp.where(t == 1, 1, jnp.where(t == 2, 3, 0)))) % 4
 
-    strip = LANES
+    strip = PB
 
     def make_slopes(p, zz):
         @pl.loop(0, PB // strip)

time: 81.9 us -> 82.2 us (level)
  no operation moved by 1% of the time
where the time goes in v3:
time: 82.2 us; the launch traced here: 82 us
  Pallas kernels  81.4 us (99%)
    pallas_call x1, Pallas kernels, shards(): pl.pallas_call(kernel, out_shape=(jax.ShapeDtypeStruct((1, 1), f32), jax....  78.7 us
    pallas_call x1, Pallas kernels, shards(): pl.pallas_call(finish, out_shape=(jax.ShapeDtypeStruct((1, 1), f32), jax....  2.7 us

profile of v3, /device:TPU:1, one launch (start us, length us, event | category | flops | bytes accessed | tf_op | source)
XLA Modules:
  0.0 82.0 jit_solution(12732248248231087882)
XLA Ops:
  0.6 78.7 %shard_map.58 = (f32[1,1]{1,0:T(1,128)}, f32[192,512]{1,0:T(8,128)}, f32[192,512]{1,0:T(8,128)}) custom-call(bf16[192,512]{1,0:T(8,128)(2,1)} %q_ref.1, bf16[192,512]{1,0:T(8,128)(2,1)} %k_ref.1, s32[1,192]{1,0:T(1,128)} %bitcast.2), custom_call_target="tpu_custom_call" | custom-call | tf_op jit(solution)/shard_map/pallas_call | solution.py:596
  79.3 2.7 %shard_map.59 = (f32[1,1]{1,0:T(1,128)}, f32[192,512]{1,0:T(8,128)}, f32[192,512]{1,0:T(8,128)}) custom-call(f32[1,1]{1,0:T(1,128)} %get-tuple-element.9.loss_in, f32[192,512]{1,0:T(8,128)} %get-tuple-element.10.query_in, f32[192,512]{1,0:T(8,128)} %get-tuple-element.11.key_in), custom_call_target="tpu_custom_call" | custom-call | tf_op jit(solution)/shard_map/pallas_call | solution.py:638

commit v4 on v2

--- a/solution.py
+++ b/solution.py
@@ -460,30 +460,31 @@
         )
         core_out(zz, yy).start()
 
-    def key_tile(zz, half):
-        cols = pl.ds(pl.multiple_of(half * PB, LANES), PB)
-        k_sum[rows(zz * CHUNK + half * PB, PB), :] = tn_dot(slopes[zz, :, cols], q_all[...])
-
-    far_half, near_half = 1 - x // 2, x // 2
-    slope_units(0, 2)
+    def key_tile(zz):
+        k_sum[rows(zz * CHUNK, CHUNK), :] = tn_dot(slopes[zz], q_all[...])
+
+    slope_units(1, 9)
+    key_tile(zlp)
+    k_first(0)
+    k_raw_up(0)
+    k_raw_down(0)
+    slope_units(0, 1)
     query_tile(0)
-    slope_units(2, 9)
+    slope_units(9, 10)
+    query_tile(1)
     add_tile(0)
     q_first(0)
-    key_tile(zlp, far_half)
-    k_first(0)
-    slope_units(9, 10)
-    query_tile(1)
     slope_units(10, 11)
     query_tile(2)
     add_tile(1)
     q_raw_up(0)
-    key_tile(zlp, near_half)
-    k_raw_up(0)
-    k_raw_down(0)
+    slope_units(11, 12)
+    query_tile(3)
     add_tile(2)
     q_raw_down(0)
-    slope_units(11, 16)
+    k_pass_up(0)
+    k_pass_down(0)
+    slope_units(12, 16)
     share = jnp.sum(positive[...], axis=0, keepdims=True) * (-2.0)
     rows_lse = row_lse[pl.ds(zh * 4 + y, 1), :]
     for g in range(PB // LANES):
@@ -502,24 +503,19 @@
     def _(o):
         loss_copy_a(o).start()
 
+    add_tile(3)
+    query_tile(4)
     q_pass_up(0)
     q_pass_down(0)
-    query_tile(4)
-    k_pass_up(0)
-    k_pass_down(0)
-    key_tile(zl, far_half)
+    key_tile(zl)
     add_tile(4)
     q_first(1)
     k_first(1)
-    query_tile(3)
-    query_tile(5)
-    add_tile(3)
-    query_tile(6)
-    add_tile(5)
-    q_raw_up(1)
-    key_tile(zl, near_half)
     k_raw_up(1)
     k_raw_down(1)
+    query_tile(5)
+    k_pair()
+    query_tile(6)
     @pl.loop(1, KC)
     def _(o):
         loss_copy_a(o).wait_recv()
@@ -533,16 +529,17 @@
     def _(o):
         loss_copy_b(o).start()
 
+    add_tile(5)
+    q_raw_up(1)
+    q_pair()
+    query_tile(7)
     add_tile(6)
     q_raw_down(1)
-    q_pair()
-    query_tile(7)
-    k_pair()
-
+
+    k_pass_up(1)
+    k_pass_down(1)
     q_pass_up(1)
     q_pass_down(1)
-    k_pass_up(1)
-    k_pass_down(1)
     add_tile(7)
 
     k_result(kg_ref)

time: 81.9 us -> 80.7 us (0.985)
  Pallas kernels: 81.1 us -> 79.9 us
    pallas_call x1, Pallas kernels: 78.4 us -> 77.2 us  [shards(): pl.pallas_call(kernel, out_shape=(jax.ShapeDtypeStruct((1, 1), f32), jax....]
where the time goes in v4:
time: 80.7 us; the launch traced here: 80.5 us
  Pallas kernels  79.9 us (99%)
    pallas_call x1, Pallas kernels, shards(): pl.pallas_call(kernel, out_shape=(jax.ShapeDtypeStruct((1, 1), f32), jax....  77.2 us
    pallas_call x1, Pallas kernels, shards(): pl.pallas_call(finish, out_shape=(jax.ShapeDtypeStruct((1, 1), f32), jax....  2.7 us

profile of v4, /device:TPU:1, one launch (start us, length us, event | category | flops | bytes accessed | tf_op | source)
XLA Modules:
  0.0 80.5 jit_solution(15990940500423469117)
XLA Ops:
  0.6 77.2 %shard_map.58 = (f32[1,1]{1,0:T(1,128)}, f32[192,512]{1,0:T(8,128)}, f32[192,512]{1,0:T(8,128)}) custom-call(bf16[192,512]{1,0:T(8,128)(2,1)} %q_ref.1, bf16[192,512]{1,0:T(8,128)(2,1)} %k_ref.1, s32[1,192]{1,0:T(1,128)} %bitcast.2), custom_call_target="tpu_custom_call" | custom-call | tf_op jit(solution)/shard_map/pallas_call | solution.py:593
  77.8 2.7 %shard_map.59 = (f32[1,1]{1,0:T(1,128)}, f32[192,512]{1,0:T(8,128)}, f32[192,512]{1,0:T(8,128)}) custom-call(f32[1,1]{1,0:T(1,128)} %get-tuple-element.9.loss_in, f32[192,512]{1,0:T(8,128)} %get-tuple-element.10.query_in, f32[192,512]{1,0:T(8,128)} %get-tuple-element.11.key_in), custom_call_target="tpu_custom_call" | custom-call | tf_op jit(solution)/shard_map/pallas_call | solution.py:635

commit v5 on v4

--- a/solution.py
+++ b/solution.py
@@ -462,6 +462,10 @@
 
     def key_tile(zz):
         k_sum[rows(zz * CHUNK, CHUNK), :] = tn_dot(slopes[zz], q_all[...])
+
+    def key_half(zz, half):
+        cols = pl.ds(pl.multiple_of(half * PB, LANES), PB)
+        k_sum[rows(zz * CHUNK + half * PB, PB), :] = tn_dot(slopes[zz, :, cols], q_all[...])
 
     slope_units(1, 9)
     key_tile(zlp)
@@ -507,10 +511,11 @@
     query_tile(4)
     q_pass_up(0)
     q_pass_down(0)
-    key_tile(zl)
+    key_half(zl, 1 - x // 2)
     add_tile(4)
     q_first(1)
     k_first(1)
+    key_half(zl, x // 2)
     k_raw_up(1)
     k_raw_down(1)
     query_tile(5)

time: 80.7 us -> 80.9 us (level)
  no operation moved by 1% of the time
where the time goes in v5:
time: 80.9 us; the launch traced here: 80.7 us
  Pallas kernels  80.1 us (99%)
    pallas_call x1, Pallas kernels, shards(): pl.pallas_call(kernel, out_shape=(jax.ShapeDtypeStruct((1, 1), f32), jax....  77.4 us
    pallas_call x1, Pallas kernels, shards(): pl.pallas_call(finish, out_shape=(jax.ShapeDtypeStruct((1, 1), f32), jax....  2.7 us

profile of v5, /device:TPU:1, one launch (start us, length us, event | category | flops | bytes accessed | tf_op | source)
XLA Modules:
  0.0 80.7 jit_solution(13579496243730057381)
XLA Ops:
  0.6 77.4 %shard_map.58 = (f32[1,1]{1,0:T(1,128)}, f32[192,512]{1,0:T(8,128)}, f32[192,512]{1,0:T(8,128)}) custom-call(bf16[192,512]{1,0:T(8,128)(2,1)} %q_ref.1, bf16[192,512]{1,0:T(8,128)(2,1)} %k_ref.1, s32[1,192]{1,0:T(1,128)} %bitcast.2), custom_call_target="tpu_custom_call" | custom-call | tf_op jit(solution)/shard_map/pallas_call | solution.py:598
  78.0 2.7 %shard_map.59 = (f32[1,1]{1,0:T(1,128)}, f32[192,512]{1,0:T(8,128)}, f32[192,512]{1,0:T(8,128)}) custom-call(f32[1,1]{1,0:T(1,128)} %get-tuple-element.9.loss_in, f32[192,512]{1,0:T(8,128)} %get-tuple-element.10.query_in, f32[192,512]{1,0:T(8,128)} %get-tuple-element.11.key_in), custom_call_target="tpu_custom_call" | custom-call | tf_op jit(solution)/shard_map/pallas_call | solution.py:640
